TPU v7x, 32 devices: a whole 2x2x4 slice. The times are simulated.
32 devices in a mesh: row: 16 (over z, x, core), col: 2 (over y).
Axes of the slice: x: 2, y: 2, z: 4, core: 2. Of those that a mesh axis runs over, the one named last changes fastest.
Arguments:
- series: float32 [2, 262144], P(None, 'row'), may hold values from -6 to 6
- exclusion: int32 [1], replicated, may hold values from 8 to 48
- col_starts: int32 [2], P('col'), may hold values from 0 to 261632, as said below
Outputs:
- row_profile: float32 [262144], P('row')
- col_profile: float32 [1024], P('col')
Inputs may be any that keep to these rules, and one draw needn't show every extreme that they name: `col_starts`: each a multiple of 512; one of them is 261632.
All inputs are finite; a program needn't handle non-finite values.
Results may differ from a plain program's by a relative error of at most 0.0014.
Values may be sent and summed in bfloat16 or wider, within the bound.
A program may use at most 64 MiB of HBM per device.

v0:
```python
import jax
import jax.numpy as jnp
from jax import lax
from jax.sharding import PartitionSpec as P

WINDOW = 64
TC = 512


def passed_along(value, axis, steps):
    count = lax.axis_size(axis)
    first, last = (max(0, -steps), min(count, count - steps))
    return lax.ppermute(value, axis, [(source, source + steps) for source in range(first, last)])


def spread_2(block, axis, source):
    block = jnp.where(lax.axis_index(axis) == source, block, jnp.zeros_like(block))
    return lax.psum(block, axis)


def normalised_columns(segment, win_count):
    channels = segment.shape[0]
    lags = segment.shape[1] - win_count + 1
    stacked = jnp.stack(
        [segment[:, lag_index : lag_index + win_count] for lag_index in range(lags)], axis=1
    )
    centred = stacked - jnp.mean(stacked, axis=1, keepdims=True)
    spread = jnp.mean(centred * centred, axis=1, keepdims=True)
    scaled = centred / jnp.sqrt(channels * lags * (spread + 1e-05))
    return scaled.reshape(channels * lags, win_count).astype(jnp.bfloat16)


def local(series, exclusion, col_starts):
    row_count = series.shape[1]
    rim_cells = passed_along(series[:, : WINDOW - 1], "row", -1)
    extended = jnp.concatenate([series, rim_cells], axis=1)
    row_windows = normalised_columns(extended, row_count)
    col_first = col_starts[0]
    owner_row = col_first // row_count
    offset = col_first - owner_row * row_count
    tile_piece = lax.dynamic_slice_in_dim(row_windows, offset, TC, 1)
    col_windows = spread_2(tile_piece, "row", owner_row)
    valid_count = row_count * lax.axis_size("row") - WINDOW + 1
    zone_width = exclusion[0]
    col_ids = col_first + jnp.arange(TC, dtype=jnp.int32)
    block_rows = min(2048, row_count)
    block_count = row_count // block_rows
    local_firsts = jnp.arange(block_count, dtype=jnp.int32) * block_rows
    device_first = lax.axis_index("row") * row_count

    def row_block_step(best_cols, local_first):
        first_row = device_first + local_first
        block = lax.dynamic_slice_in_dim(row_windows, local_first, block_rows, 1)
        scores = lax.dot_general(
            block, col_windows, (((0,), (0,)), ((), ())), preferred_element_type=jnp.float32
        )
        row_ids = first_row + jnp.arange(block_rows, dtype=jnp.int32)
        kept_mask = (col_ids[None, :] - row_ids[:, None] >= zone_width) & (col_ids < valid_count)[
            None, :
        ]
        masked = jnp.where(kept_mask, scores, jnp.float32(-1.0))
        row_part = jnp.max(masked, axis=1)
        col_part = jnp.max(masked, axis=0)
        return (jnp.maximum(best_cols, col_part), row_part)

    start_best = jnp.full((TC,), -1.0, jnp.float32)
    best_cols, row_parts = lax.scan(row_block_step, start_best, local_firsts)
    row_best = row_parts.reshape(row_count)
    col_profile = lax.pmax(best_cols, "row")
    row_profile = lax.pmax(row_best, "col")
    return (row_profile, col_profile)


def solution(mesh):
    placed = (P(None, "row"), P(), P("col"))
    return jax.shard_map(
        local, mesh=mesh, in_specs=placed, out_specs=(P("row"), P("col")), check_vma=False
    )
```

profile of v0, /device:TPU:0, one launch (start us, length us, event | category | flops | bytes accessed | tf_op | source)
XLA Modules:
  0.0 297.7 jit_solution(7765061848753870517)
XLA Ops:
  7.9 1.3 collective-permute-start
  9.2 0.9 constant_dynamic-update-slice_fusion.1
  10.1 1.6 constant_dynamic-update-slice_fusion.65
  12.4 9.8 %add_multiply_fusion = f32[2,16384]{1,0:T(2,128)S(1)} fusion(f32[2,16384]{1,0:T(2,128)} %param.5, f32[2,16447]{1,0:T(2,128)S(1)} %constant_dynamic-update-slice_fusion), kind=kLoop, calls=%fused_computation.80 | loop fusion | flops 2097152 | bytes 8519680 | tf_op jit(solution)/shard_map/div | solution.py:27
  23.1 0.9 constant_dynamic-update-slice_fusion.63
  27.3 0.9 constant_dynamic-update-slice_fusion.58
  57.1 0.9 constant_dynamic-update-slice_fusion.23
  75.0 0.9 constant_dynamic-update-slice_fusion.2
  75.9 8.0 %multiply_reduce_fusion = f32[2,16384]{1,0:T(2,128)S(1)} fusion(f32[2,64,16384]{2,0,1:T(2,128)} %constant_dynamic-update-slice_fusion.2, f32[2,16384]{1,0:T(2,128)S(1)} %add_multiply_fusion), kind=kLoop, calls=%fused_computation.10 | loop fusion | flops 6258688 | bytes 8650752 | tf_op jit(solution)/shard_map/reduce_sum | solution.py:28
  84.1 10.3 %divide_convert_fusion = bf16[2,64,16384]{2,0,1:T(2,128)(2,1)} fusion(f32[2,64,16384]{2,0,1:T(2,128)} %constant_dynamic-update-slice_fusion.2, f32[2,16384]{1,0:T(2,128)S(1)} %multiply_sqrt_fusion, f32[2,16384]{1,0:T(2,128)S(1)} %add_multiply_fusion), kind=kLoop, calls=%fused_computation.11 | loop fusion | flops 6291456 | bytes 12845056 | tf_op jit(solution)/shard_map/convert_element_type | solution.py:30
  94.4 4.5 %copy.5 = bf16[2,64,16384]{2,1,0:T(8,128)(2,1)S(1)} copy(bf16[2,64,16384]{2,0,1:T(2,128)(2,1)} %divide_convert_fusion) | data formatting | bytes 8388608 | tf_op jit(solution)/shard_map/convert_element_type | solution.py:30
  98.9 1.9 copy-done
  101.6 90.5 %all-reduce.3.cloned.1.call-done = bf16[128,512]{1,0:T(8,128)(2,1)} async-done(((bf16[128,512]{1,0:T(8,128)(2,1)}), bf16[128,512]{1,0:T(8,128)(2,1)}) %all-reduce.3.cloned.1.call-update) | async-done | bytes 131088 | tf_op jit(solution)/shard_map/psum | solution.py:18
  192.2 64.3 %while.13 = (s32[]{:T(128)}, f32[512]{0:T(512)S(1)}, f32[8,2048]{1,0:T(8,128)S(1)}, s32[8]{0:T(128)S(1)}, s32[]{:T(128)}, /*index=5*/s32[]{:T(128)}, bf16[128,16...) while((s32[]{:T(128)}, f32[512]{0:T(512)S(1)}, ...), condition=%wide.region_5.6_spmd.clone, body=%wide.region_2.5_spmd.clone.sunk | while | flops 274728960 | bytes 710349 | solution.py:67
  196.5 3.4 %fusion.11 = (f32[2048]{0:T(1024)S(1)}, f32[512]{0:T(512)S(1)}) fusion(bf16[128,512]{1,0:T(8,128)(2,1)} %get-tuple-element.195, bf16[128,16384]{1,0:T(8,128)(2,1)} %get-tuple-element.194, s32[]{:T(128)S(6)} %select_n.33, pred[512]{0:T(512)(128)(4,1)S(1)} %broadcast_compare_fusion.2, s32[]{:T(128)} %get-tuple-element.193, ...), kind=kOutput, calls=%fused_computation.82.clone.1 | convolution fusion | flops 274724352 | bytes 676868 | tf_op jit(solution)/shard_map/while/body/eval_jaxpr/dot_general | solution.py:54
  204.6 3.4 %fusion.11 = (f32[2048]{0:T(1024)S(1)}, f32[512]{0:T(512)S(1)}) fusion(bf16[128,512]{1,0:T(8,128)(2,1)} %get-tuple-element.195, bf16[128,16384]{1,0:T(8,128)(2,1)} %get-tuple-element.194, s32[]{:T(128)S(6)} %select_n.33, pred[512]{0:T(512)(128)(4,1)S(1)} %broadcast_compare_fusion.2, s32[]{:T(128)} %get-tuple-element.193, ...), kind=kOutput, calls=%fused_computation.82.clone.1 | convolution fusion | flops 274724352 | bytes 676868 | tf_op jit(solution)/shard_map/while/body/eval_jaxpr/dot_general | solution.py:54
  212.6 3.4 %fusion.11 = (f32[2048]{0:T(1024)S(1)}, f32[512]{0:T(512)S(1)}) fusion(bf16[128,512]{1,0:T(8,128)(2,1)} %get-tuple-element.195, bf16[128,16384]{1,0:T(8,128)(2,1)} %get-tuple-element.194, s32[]{:T(128)S(6)} %select_n.33, pred[512]{0:T(512)(128)(4,1)S(1)} %broadcast_compare_fusion.2, s32[]{:T(128)} %get-tuple-element.193, ...), kind=kOutput, calls=%fused_computation.82.clone.1 | convolution fusion | flops 274724352 | bytes 676868 | tf_op jit(solution)/shard_map/while/body/eval_jaxpr/dot_general | solution.py:54
  220.6 3.4 %fusion.11 = (f32[2048]{0:T(1024)S(1)}, f32[512]{0:T(512)S(1)}) fusion(bf16[128,512]{1,0:T(8,128)(2,1)} %get-tuple-element.195, bf16[128,16384]{1,0:T(8,128)(2,1)} %get-tuple-element.194, s32[]{:T(128)S(6)} %select_n.33, pred[512]{0:T(512)(128)(4,1)S(1)} %broadcast_compare_fusion.2, s32[]{:T(128)} %get-tuple-element.193, ...), kind=kOutput, calls=%fused_computation.82.clone.1 | convolution fusion | flops 274724352 | bytes 676868 | tf_op jit(solution)/shard_map/while/body/eval_jaxpr/dot_general | solution.py:54
  228.7 3.4 %fusion.11 = (f32[2048]{0:T(1024)S(1)}, f32[512]{0:T(512)S(1)}) fusion(bf16[128,512]{1,0:T(8,128)(2,1)} %get-tuple-element.195, bf16[128,16384]{1,0:T(8,128)(2,1)} %get-tuple-element.194, s32[]{:T(128)S(6)} %select_n.33, pred[512]{0:T(512)(128)(4,1)S(1)} %broadcast_compare_fusion.2, s32[]{:T(128)} %get-tuple-element.193, ...), kind=kOutput, calls=%fused_computation.82.clone.1 | convolution fusion | flops 274724352 | bytes 676868 | tf_op jit(solution)/shard_map/while/body/eval_jaxpr/dot_general | solution.py:54
  236.7 3.4 %fusion.11 = (f32[2048]{0:T(1024)S(1)}, f32[512]{0:T(512)S(1)}) fusion(bf16[128,512]{1,0:T(8,128)(2,1)} %get-tuple-element.195, bf16[128,16384]{1,0:T(8,128)(2,1)} %get-tuple-element.194, s32[]{:T(128)S(6)} %select_n.33, pred[512]{0:T(512)(128)(4,1)S(1)} %broadcast_compare_fusion.2, s32[]{:T(128)} %get-tuple-element.193, ...), kind=kOutput, calls=%fused_computation.82.clone.1 | convolution fusion | flops 274724352 | bytes 676868 | tf_op jit(solution)/shard_map/while/body/eval_jaxpr/dot_general | solution.py:54
  244.7 3.4 %fusion.11 = (f32[2048]{0:T(1024)S(1)}, f32[512]{0:T(512)S(1)}) fusion(bf16[128,512]{1,0:T(8,128)(2,1)} %get-tuple-element.195, bf16[128,16384]{1,0:T(8,128)(2,1)} %get-tuple-element.194, s32[]{:T(128)S(6)} %select_n.33, pred[512]{0:T(512)(128)(4,1)S(1)} %broadcast_compare_fusion.2, s32[]{:T(128)} %get-tuple-element.193, ...), kind=kOutput, calls=%fused_computation.82.clone.1 | convolution fusion | flops 274724352 | bytes 676868 | tf_op jit(solution)/shard_map/while/body/eval_jaxpr/dot_general | solution.py:54
  252.8 3.4 %fusion.11 = (f32[2048]{0:T(1024)S(1)}, f32[512]{0:T(512)S(1)}) fusion(bf16[128,512]{1,0:T(8,128)(2,1)} %get-tuple-element.195, bf16[128,16384]{1,0:T(8,128)(2,1)} %get-tuple-element.194, s32[]{:T(128)S(6)} %select_n.33, pred[512]{0:T(512)(128)(4,1)S(1)} %broadcast_compare_fusion.2, s32[]{:T(128)} %get-tuple-element.193, ...), kind=kOutput, calls=%fused_computation.82.clone.1 | convolution fusion | flops 274724352 | bytes 676868 | tf_op jit(solution)/shard_map/while/body/eval_jaxpr/dot_general | solution.py:54
  257.1 32.3 %pmax.15 = f32[512]{0:T(512)} all-reduce(f32[512]{0:T(512)S(1)} %get-tuple-element.51), channel_id=1, replica_groups=mesh['row'=16,'col'=2] {'row'}, use_global_device_ids=true, to_apply=%region_7.8 | all-reduce | flops 512 | bytes 4096 | tf_op jit(solution)/shard_map/pmax | solution.py:69
  289.4 1.5 copy.84
  (122 shorter events, 69.7 us)
Async XLA Ops:
  7.2 185.0 %all-reduce.3.cloned.1.call-start = ((), (), s32[]{:S(2)}) async-start(), calls=%async_computation | async-start | bytes 262144 | tf_op jit(solution)/shard_map/psum | solution.py:18
  7.9 4.5 %collective-permute-start = (f32[2,63]{1,0:T(2,128)S(1)}, f32[2,63]{1,0:T(2,128)S(1)}, u32[]{:S(2)}, u32[]{:S(2)}) collective-permute-start(f32[2,63]{1,0:T(2,128)S(1)} %slice.192), channel_id=1, source_target_pairs={{2,0},{4,2},{6,4},{8,6},{10,8},{12,10},{14,12},{16,14},{18,16},{20... | collective-permute-start | bytes 1520 | tf_op jit(solution)/shard_map/ppermute | solution.py:13
  98.9 1.9 copy-start
  101.6 187.8 %all-reduce.5.cloned.1.call-start = ((), (), s32[]{:S(2)}) async-start(), calls=%async_computation.1 | async-start | bytes 131072 | tf_op jit(solution)/shard_map/pmax | solution.py:70
Sparse Core Ops, SparseCore 0:
  101.7 90.4 all-reduce.2
  257.2 22.4 all-reduce.4
where the time goes:
time: 299 us; the launch traced here: 298 us
  waiting for transfers between devices  90.6 us (30%)
  local copies, waits for them, and re-layouts  71.9 us (24%)
  other arithmetic  39.6 us (13%)
  blocking collectives  32.3 us (11%)
  matrix products  27.3 us (9%)
  loops' own time  19.9 us (7%)
  between operations  14.8 us (5%)
    psum x1, waiting for transfers between devices, spread_2(): return lax.psum(block, axis)  90.5 us
    unnamed x68, local copies, waits for them, and re-layouts  59.3 us
    pmax x1, blocking collectives, local(): col_profile = lax.pmax(best_cols, 'row')  32.3 us
    dot_general x8, matrix products, row_block_step(): lax.dot_general(block, col_windows, (((0,), (0,)), ((), ())), preferred_e...  27.3 us
    another operation x1, loops' own time, local(): best_cols, row_parts = lax.scan(row_block_step, start_best, local_firsts)  19.9 us
    convert_element_type x1, other arithmetic, normalised_columns(): return scaled.reshape(channels * lags, win_count).astype(jnp.bfloat16)  10.3 us
    div x1, other arithmetic, normalised_columns(): centred = stacked - jnp.mean(stacked, axis=1, keepdims=True)  9.81 us
    reduce_sum x1, other arithmetic, normalised_columns(): spread = jnp.mean(centred * centred, axis=1, keepdims=True)  8.04 us
  transfers between devices with their start and end apart: 3, of which 1 were waited for; matrix products, arithmetic and copies ran while one was open for 1% of the time, Pallas kernels for 0%

commit v1 on v0

v1 whole, which is shorter than its diff:
```python
import functools

import jax
import jax.numpy as jnp
from jax import lax
from jax.experimental import pallas as pl
from jax.experimental.pallas import tpu as pltpu
from jax.sharding import PartitionSpec as P

WINDOW = 64
TC = 512
LANES = 128
CHUNK = TC
EDGE = TC + LANES
SPAN = EDGE + LANES
MASKED = -4.0
MESH = pl.DeviceIdType.MESH


def normalised(x, count):
    channels, length = x.shape
    parts = []
    for channel in range(channels):
        line = jnp.broadcast_to(x[channel : channel + 1], (8, length))
        fan = pltpu.roll(line, length - 7, 1, stride=1, stride_axis=0)
        groups = [fan[:, 8 * g : 8 * g + count] for g in range(WINDOW // 8)]
        total = functools.reduce(jnp.add, groups)
        mean = jnp.sum(total, axis=0, keepdims=True) * (1.0 / WINDOW)
        groups = [g - mean for g in groups]
        square = functools.reduce(jnp.add, [g * g for g in groups])
        spread = jnp.sum(square, axis=0, keepdims=True) * (1.0 / WINDOW)
        scale = 1.0 / jnp.sqrt(channels * WINDOW * (spread + 1e-05))
        parts += [g * scale for g in groups]
    return jnp.concatenate(parts, axis=0)


def kernel(
    R, C, N, pieces,
    series, exclusion, col_starts,
    row_out, col_out,
    seg_all, row_all, col_all, rows, cols, edge, best,
    seg_send, seg_recv, col_send, col_recv, row_send, row_recv,
):
    r, c = lax.axis_index("row"), lax.axis_index("col")
    barrier = pltpu.get_barrier_semaphore()

    @pl.loop(1, R)
    def _(d):
        pl.semaphore_signal(
            barrier, inc=1, device_id=(lax.rem(r + d, R), c), device_id_type=MESH
        )

    @pl.loop(1, C)
    def _(d):
        pl.semaphore_signal(
            barrier, inc=1, device_id=(r, lax.rem(c + d, C)), device_id_type=MESH
        )

    col_first = col_starts[0]
    start = col_first - r * N

    before = jnp.zeros((2, LANES), jnp.float32)
    body = jnp.zeros((2, TC), jnp.float32)
    after = jnp.zeros((2, LANES), jnp.float32)
    for first in range(0, N, TC):
        part = series[:, first : first + TC]
        away = jnp.full((2, TC), start - first)
        body = jnp.where(away == 0, part, body)
        before = jnp.where(away[:, :LANES] == TC, part[:, TC - LANES :], before)
        after = jnp.where(away[:, :LANES] == -TC, part[:, :LANES], after)
    seg_all[r, :, 0:LANES] = before
    seg_all[r, :, LANES : LANES + TC] = body
    seg_all[r, :, LANES + TC : SPAN] = after
    seg_all[r, :, SPAN:] = series[:, 0:LANES]
    pl.semaphore_wait(barrier, R + C - 2)

    def seg_copy(d):
        return pltpu.make_async_remote_copy(
            src_ref=seg_all.at[r], dst_ref=seg_all.at[r],
            send_sem=seg_send.at[d], recv_sem=seg_recv.at[d],
            device_id=(lax.rem(r + d, R), c), device_id_type=MESH,
        )

    def col_copy(d):
        return pltpu.make_async_remote_copy(
            src_ref=col_all.at[r], dst_ref=col_all.at[r],
            send_sem=col_send.at[d], recv_sem=col_recv.at[d],
            device_id=(lax.rem(r + d, R), c), device_id_type=MESH,
        )

    span = N // pieces

    def row_copy(d, piece):
        part = row_all.at[c, :, pl.ds(piece * span, span)]
        return pltpu.make_async_remote_copy(
            src_ref=part, dst_ref=part,
            send_sem=row_send.at[d, piece], recv_sem=row_recv.at[d, piece],
            device_id=(r, lax.rem(c + d, C)), device_id_type=MESH,
        )

    @pl.loop(1, R)
    def _(d):
        seg_copy(d).start()

    @pl.loop(0, N // CHUNK - 1)
    def _(step):
        first = pl.multiple_of(step * CHUNK, CHUNK)
        block = normalised(series[:, pl.ds(first, CHUNK + LANES)], CHUNK)
        rows[:, pl.ds(first, CHUNK)] = block.astype(jnp.bfloat16)

    @pl.loop(1, R)
    def _(d):
        seg_copy(d).wait()

    rim = seg_all[lax.rem(r + 1, R), :, SPAN:]
    rim = jnp.where(r == R - 1, 0.0, rim)
    tail = jnp.concatenate([series[:, N - CHUNK :], rim], axis=1)
    rows[:, N - CHUNK :] = normalised(tail, CHUNK).astype(jnp.bfloat16)

    around = normalised(jnp.sum(seg_all[:, :, :SPAN], axis=0), EDGE)
    cols[:, :LANES] = around[:, LANES:].T.astype(jnp.bfloat16)
    around = around.astype(jnp.bfloat16)
    place = col_first + lax.broadcasted_iota(jnp.int32, (TC, LANES), 0)
    last = jnp.where(place <= R * N - WINDOW, place - exclusion[0], -1)
    lane = lax.broadcasted_iota(jnp.int32, (TC, LANES), 1)
    cut = jnp.where(lane * LANES + (r * N + LANES - 1) > last, MASKED, 0.0)
    cols[:, LANES:] = cut.astype(jnp.bfloat16)

    col_best = jnp.full((TC, LANES), -1.0, jnp.float32)
    edges = []
    for g in range(EDGE // LANES):
        block = around[:, g * LANES : (g + 1) * LANES]
        scores = jnp.dot(cols[:, :LANES], block, preferred_element_type=jnp.float32)
        row = col_first + ((g - 1) * LANES) + lane
        scores = jnp.where((row <= last) & (row >= 0), scores, -1.0)
        col_best = jnp.maximum(col_best, scores)
        edges.append(jnp.max(scores, axis=0, keepdims=True))
    best[...] = col_best
    low = jnp.full((1, CHUNK - LANES), -1.0, jnp.float32)
    edge[0] = jnp.concatenate(edges[1:], axis=1)
    edge[1] = jnp.concatenate([low, edges[0]], axis=1)

    group = lax.broadcasted_iota(jnp.int32, (LANES, CHUNK), 0)
    owned = lax.broadcasted_iota(jnp.int32, (LANES, CHUNK), 1) // LANES

    def step_rows(step):
        first = pl.multiple_of(step * CHUNK, CHUNK)
        mark = jnp.where(group - owned == step * (CHUNK // LANES), 1.0, 0.0)
        right = jnp.concatenate([rows[:, pl.ds(first, CHUNK)], mark.astype(jnp.bfloat16)], axis=0)
        scores = jnp.dot(cols[...], right, preferred_element_type=jnp.float32)
        part = scores[:, :LANES]
        for g in range(1, CHUNK // LANES):
            part = jnp.maximum(part, scores[:, g * LANES : (g + 1) * LANES])
        best[...] = jnp.maximum(best[...], part)
        row_best = jnp.max(scores, axis=0, keepdims=True)
        away = jnp.full((1, CHUNK), col_starts[0] - r * N - first)
        row_best = jnp.maximum(row_best, jnp.where(away == 0, edge[0], -1.0))
        row_best = jnp.maximum(row_best, jnp.where(away == CHUNK, edge[1], -1.0))
        row_all[c, :, pl.ds(first, CHUNK)] = row_best

    per_piece = N // CHUNK // pieces
    for piece in range(pieces):
        pl.loop(piece * per_piece, (piece + 1) * per_piece)(step_rows)

        @pl.loop(1, C)
        def _(d):
            row_copy(d, piece).start()

    col_all[r] = jnp.max(best[...].T, axis=0, keepdims=True)

    @pl.loop(1, R)
    def _(d):
        col_copy(d).start()

    @pl.loop(1, C)
    def _(d):
        for piece in range(pieces):
            row_copy(d, piece).wait()

    row_out[...] = functools.reduce(jnp.maximum, [row_all[k] for k in range(C)])

    @pl.loop(1, R)
    def _(d):
        col_copy(d).wait()

    col_out[...] = jnp.max(col_all[...], axis=0)


def local(R, C, series, exclusion, col_starts):
    channels, N = series.shape
    pieces = 4
    vmem, smem = pl.BlockSpec(memory_space=pltpu.VMEM), pl.BlockSpec(memory_space=pltpu.SMEM)
    dma = pltpu.SemaphoreType.DMA
    row_best, col_best = pl.pallas_call(
        functools.partial(kernel, R, C, N, pieces),
        out_shape=(
            jax.ShapeDtypeStruct((1, N), jnp.float32),
            jax.ShapeDtypeStruct((1, TC), jnp.float32),
        ),
        in_specs=[vmem, smem, smem],
        out_specs=(vmem, vmem),
        scratch_shapes=[
            pltpu.VMEM((R, channels, SPAN + LANES), jnp.float32),
            pltpu.VMEM((C, 1, N), jnp.float32),
            pltpu.VMEM((R, 1, TC), jnp.float32),
            pltpu.VMEM((channels * WINDOW, N), jnp.bfloat16),
            pltpu.VMEM((TC, 2 * LANES), jnp.bfloat16),
            pltpu.VMEM((2, 1, CHUNK), jnp.float32),
            pltpu.VMEM((TC, LANES), jnp.float32),
            dma((R,)), dma((R,)), dma((R,)), dma((R,)),
            dma((C, pieces)), dma((C, pieces)),
        ],
        compiler_params=pltpu.CompilerParams(
            collective_id=0, has_side_effects=True, vmem_limit_bytes=40 * 1024 * 1024
        ),
    )(series, exclusion, col_starts)
    return row_best.reshape(N), col_best.reshape(TC)


def solution(mesh):
    placed = (P(None, "row"), P(), P("col"))
    R, C = mesh.shape["row"], mesh.shape["col"]
    return jax.shard_map(
        functools.partial(local, R, C),
        mesh=mesh,
        in_specs=placed,
        out_specs=(P("row"), P("col")),
        check_vma=False,
    )
```

time: 299 us -> 46.2 us (0.15)
  waiting for transfers between devices: 90.6 us -> 0 us
  local copies, waits for them, and re-layouts: 71.9 us -> 2.11 us
  Pallas kernels: 0 us -> 42 us
  other arithmetic: 39.6 us -> 0 us
  blocking collectives: 32.3 us -> 0 us
  matrix products: 27.3 us -> 0 us
  loops' own time: 19.9 us -> 0 us
  between operations: 14.8 us -> 1.94 us
    psum x1 -> x0, waiting for transfers between devices: 90.5 us -> none  [spread_2(): return lax.psum(block, axis)]
    unnamed x68 -> x4, local copies, waits for them, and re-layouts: 59.3 us -> 2.11 us
    pallas_call x0 -> x1, Pallas kernels: none -> 42 us  [local(): pl.pallas_call(functools.partial(kernel, R, C, N, pieces), out_shape=(jax...]
    pmax x1 -> x0, blocking collectives: 32.3 us -> none  [local(): col_profile = lax.pmax(best_cols, 'row')]
    dot_general x8 -> x0, matrix products: 27.3 us -> none  [row_block_step(): lax.dot_general(block, col_windows, (((0,), (0,)), ((), ())), preferred_e...]
    another operation x1 -> x0, loops' own time: 19.9 us -> none  [local(): best_cols, row_parts = lax.scan(row_block_step, start_best, local_firsts)]
    convert_element_type x1 -> x0, other arithmetic: 10.3 us -> none  [normalised_columns(): return scaled.reshape(channels * lags, win_count).astype(jnp.bfloat16)]
    div x1 -> x0, other arithmetic: 9.81 us -> none  [normalised_columns(): centred = stacked - jnp.mean(stacked, axis=1, keepdims=True)]
  transfers between devices with their start and end apart: 3 -> 0, of which waited for: 1 -> 0; matrix products, arithmetic and copies ran while one was open for 1% -> 0% of each run, Pallas kernels for 0% -> 0%
where the time goes in v1:
time: 46.2 us; the launch traced here: 46 us
  Pallas kernels  42 us (91%)
  local copies, waits for them, and re-layouts  2.11 us (5%)
  between operations  1.94 us (4%)
    pallas_call x1, Pallas kernels, local(): pl.pallas_call(functools.partial(kernel, R, C, N, pieces), out_shape=(jax...  42 us
    unnamed x4, local copies, waits for them, and re-layouts  2.11 us

profile of v1, /device:TPU:0, one launch (start us, length us, event | category | flops | bytes accessed | tf_op | source)
XLA Modules:
  0.0 46.0 jit_solution(9533730226230063813)
XLA Ops:
  1.9 0.0 copy-start
  1.9 0.9 %copy-done = f32[2,16384]{1,0:T(2,128)S(1)} copy-done((f32[2,16384]{1,0:T(2,128)S(1)}, f32[2,16384]{1,0:T(2,128)}, u32[]{:S(2)}) %copy-start) | copy-done | bytes 131096
  2.8 42.0 %shard_map.50 = (f32[1,16384]{1,0:T(1,128)S(1)}, f32[1,512]{1,0:T(1,128)S(1)}) custom-call(f32[2,16384]{1,0:T(2,128)S(1)} %copy-done, s32[1]{0:T(128)S(6)} %copy.7.exclusion, s32[1]{0:T(128)S(6)} %copy.8.col_starts), custom_call_target="tpu_custom_call" | custom-call | tf_op jit(solution)/shard_map/pallas_call | solution.py:194
  44.8 0.6 %copy.9 = f32[16384]{0:T(1024)} copy(f32[16384]{0:T(1024)S(1)} %bitcast.2) | data formatting | bytes 131072
  45.5 0.6 %copy.10 = f32[512]{0:T(512)} copy(f32[512]{0:T(512)S(1)} %bitcast.3) | data formatting | bytes 4096
Async XLA Ops:
  1.9 0.9 %copy-start = (f32[2,16384]{1,0:T(2,128)S(1)}, f32[2,16384]{1,0:T(2,128)}, u32[]{:S(2)}) copy-start(f32[2,16384]{1,0:T(2,128)} %series.1) | copy-start | bytes 393220

commit v2 on v1

--- a/solution.py
+++ b/solution.py
@@ -22,8 +22,10 @@
     parts = []
     for channel in range(channels):
         line = jnp.broadcast_to(x[channel : channel + 1], (8, length))
-        fan = pltpu.roll(line, length - 7, 1, stride=1, stride_axis=0)
-        groups = [fan[:, 8 * g : 8 * g + count] for g in range(WINDOW // 8)]
+        groups = [
+            pltpu.roll(line, length - 7 - 8 * g, 1, stride=1, stride_axis=0)[:, :count]
+            for g in range(WINDOW // 8)
+        ]
         total = functools.reduce(jnp.add, groups)
         mean = jnp.sum(total, axis=0, keepdims=True) * (1.0 / WINDOW)
         groups = [g - mean for g in groups]
@@ -102,11 +104,20 @@
     def _(d):
         seg_copy(d).start()
 
-    @pl.loop(0, N // CHUNK - 1)
-    def _(step):
-        first = pl.multiple_of(step * CHUNK, CHUNK)
+    def rows_of(step):
+        first = step * CHUNK if isinstance(step, int) else pl.multiple_of(step * CHUNK, CHUNK)
         block = normalised(series[:, pl.ds(first, CHUNK + LANES)], CHUNK)
         rows[:, pl.ds(first, CHUNK)] = block.astype(jnp.bfloat16)
+
+    whole = (N // CHUNK - 1) // 2
+
+    @pl.loop(0, whole)
+    def _(step):
+        for k in range(2):
+            rows_of(step * 2 + k)
+
+    for k in range(whole * 2, N // CHUNK - 1):
+        rows_of(k)
 
     @pl.loop(1, R)
     def _(d):
@@ -160,7 +171,11 @@
 
     per_piece = N // CHUNK // pieces
     for piece in range(pieces):
-        pl.loop(piece * per_piece, (piece + 1) * per_piece)(step_rows)
+        @pl.loop(0, per_piece // 4)
+        def _(step):
+            for k in range(4):
+                step_rows(piece * per_piece + step * 4 + k)
+
 
         @pl.loop(1, C)
         def _(d):

time: 46.2 us -> 26.9 us (0.58)
  Pallas kernels: 42 us -> 22.7 us
    pallas_call x1, Pallas kernels: 42 us -> 22.7 us  [local(): pl.pallas_call(functools.partial(kernel, R, C, N, pieces), out_shape=(jax...]
where the time goes in v2:
time: 26.9 us; the launch traced here: 26.7 us
  Pallas kernels  22.7 us (84%)
  local copies, waits for them, and re-layouts  2.11 us (8%)
  between operations  1.94 us (7%)
    pallas_call x1, Pallas kernels, local(): pl.pallas_call(functools.partial(kernel, R, C, N, pieces), out_shape=(jax...  22.7 us
    unnamed x4, local copies, waits for them, and re-layouts  2.11 us

profile of v2, /device:TPU:0, one launch (start us, length us, event | category | flops | bytes accessed | tf_op | source)
XLA Modules:
  0.0 26.7 jit_solution(17397877775973101719)
XLA Ops:
  1.9 0.0 copy-start
  1.9 0.9 %copy-done = f32[2,16384]{1,0:T(2,128)S(1)} copy-done((f32[2,16384]{1,0:T(2,128)S(1)}, f32[2,16384]{1,0:T(2,128)}, u32[]{:S(2)}) %copy-start) | copy-done | bytes 131096
  2.8 22.7 %shard_map.50 = (f32[1,16384]{1,0:T(1,128)S(1)}, f32[1,512]{1,0:T(1,128)S(1)}) custom-call(f32[2,16384]{1,0:T(2,128)S(1)} %copy-done, s32[1]{0:T(128)S(6)} %copy.7.exclusion, s32[1]{0:T(128)S(6)} %copy.8.col_starts), custom_call_target="tpu_custom_call" | custom-call | tf_op jit(solution)/shard_map/pallas_call | solution.py:209
  25.5 0.6 %copy.9 = f32[16384]{0:T(1024)} copy(f32[16384]{0:T(1024)S(1)} %bitcast.2) | data formatting | bytes 131072
  26.1 0.6 %copy.10 = f32[512]{0:T(512)} copy(f32[512]{0:T(512)S(1)} %bitcast.3) | data formatting | bytes 4096
Async XLA Ops:
  1.9 0.9 %copy-start = (f32[2,16384]{1,0:T(2,128)S(1)}, f32[2,16384]{1,0:T(2,128)}, u32[]{:S(2)}) copy-start(f32[2,16384]{1,0:T(2,128)} %series.1) | copy-start | bytes 393220

commit v3 on v2

--- a/solution.py
+++ b/solution.py
@@ -170,11 +170,12 @@
         row_all[c, :, pl.ds(first, CHUNK)] = row_best
 
     per_piece = N // CHUNK // pieces
+    unit = 8 if per_piece % 8 == 0 else 1
     for piece in range(pieces):
-        @pl.loop(0, per_piece // 4)
+        @pl.loop(0, per_piece // unit)
         def _(step):
-            for k in range(4):
-                step_rows(piece * per_piece + step * 4 + k)
+            for k in range(unit):
+                step_rows(piece * per_piece + step * unit + k)
 
 
         @pl.loop(1, C)

time: 26.9 us -> 25.8 us (0.959)
  Pallas kernels: 22.7 us -> 21.6 us
    pallas_call x1, Pallas kernels: 22.7 us -> 21.6 us  [local(): pl.pallas_call(functools.partial(kernel, R, C, N, pieces), out_shape=(jax...]
where the time goes in v3:
time: 25.8 us; the launch traced here: 25.6 us
  Pallas kernels  21.6 us (84%)
  local copies, waits for them, and re-layouts  2.11 us (8%)
  between operations  1.94 us (8%)
    pallas_call x1, Pallas kernels, local(): pl.pallas_call(functools.partial(kernel, R, C, N, pieces), out_shape=(jax...  21.6 us
    unnamed x4, local copies, waits for them, and re-layouts  2.11 us

profile of v3, /device:TPU:0, one launch (start us, length us, event | category | flops | bytes accessed | tf_op | source)
XLA Modules:
  0.0 25.6 jit_solution(1818033452027548315)
XLA Ops:
  1.9 0.0 copy-start
  1.9 0.9 %copy-done = f32[2,16384]{1,0:T(2,128)S(1)} copy-done((f32[2,16384]{1,0:T(2,128)S(1)}, f32[2,16384]{1,0:T(2,128)}, u32[]{:S(2)}) %copy-start) | copy-done | bytes 131096
  2.8 21.6 %shard_map.50 = (f32[1,16384]{1,0:T(1,128)S(1)}, f32[1,512]{1,0:T(1,128)S(1)}) custom-call(f32[2,16384]{1,0:T(2,128)S(1)} %copy-done, s32[1]{0:T(128)S(6)} %copy.7.exclusion, s32[1]{0:T(128)S(6)} %copy.8.col_starts), custom_call_target="tpu_custom_call" | custom-call | tf_op jit(solution)/shard_map/pallas_call | solution.py:210
  24.4 0.6 %copy.9 = f32[16384]{0:T(1024)} copy(f32[16384]{0:T(1024)S(1)} %bitcast.2) | data formatting | bytes 131072
  25.0 0.6 %copy.10 = f32[512]{0:T(512)} copy(f32[512]{0:T(512)S(1)} %bitcast.3) | data formatting | bytes 4096
Async XLA Ops:
  1.9 0.9 %copy-start = (f32[2,16384]{1,0:T(2,128)S(1)}, f32[2,16384]{1,0:T(2,128)}, u32[]{:S(2)}) copy-start(f32[2,16384]{1,0:T(2,128)} %series.1) | copy-start | bytes 393220
